TPU v7x, 32 devices: a whole 2x2x4 slice. The times are simulated.
32 devices in a mesh: dp: 16 (over z, y, core), seq: 2 (over x).
Axes of the slice: x: 2, y: 2, z: 4, core: 2. Of those that a mesh axis runs over, the one named last changes fastest.
Arguments:
- tokens: bfloat16 [32, 1024, 1152], P('dp', 'seq'), may hold values from -6 to 6
- cotangent: bfloat16 [32, 1024, 1152], P('dp', 'seq'), may hold values from -6 to 6
- lengths: int32 [32, 10], P('dp'), may hold values from 0 to 1024, as said below
- adapter_ids: int32 [32, 10], P('dp'), may hold values from 0 to 7
- w_query: bfloat16 [1152, 1152], P('dp', 'seq'), may hold values from -0.1875 to 0.1875
- w_key: bfloat16 [1152, 1152], P('dp', 'seq'), may hold values from -0.1875 to 0.1875
- w_value: bfloat16 [1152, 1152], P('dp', 'seq'), may hold values from -0.1875 to 0.1875
- w_out: bfloat16 [1152, 1152], P('dp', 'seq'), may hold values from -2 to 2
- w_up: bfloat16 [1152, 4304], P('dp', 'seq'), may hold values from -0.1875 to 0.1875
- w_down: bfloat16 [4304, 1152], P('seq', 'dp'), may hold values from -0.09375 to 0.09375
- b_query: bfloat16 [1152], P('seq'), may hold values from -3 to 3
- b_value: bfloat16 [1152], P('seq'), may hold values from -0.29882812 to 0.29882812
- b_out: bfloat16 [1152], P('seq'), may hold values from -1.796875 to 1.796875
- b_up: bfloat16 [4304], P('seq'), may hold values from -3 to 3
- b_down: bfloat16 [1152], P('seq'), may hold values from -1.796875 to 1.796875
- gain_one: bfloat16 [1152], P('seq'), may hold values from 0.5 to 1.5
- shift_one: bfloat16 [1152], P('seq'), may hold values from -1.796875 to 1.796875
- gain_two: bfloat16 [1152], P('seq'), may hold values from 0.5 to 1.5
- shift_two: bfloat16 [1152], P('seq'), may hold values from -1.796875 to 1.796875
- qkv_a: bfloat16 [3, 8, 1152, 16], P(None, 'seq'), may hold values from -0.1875 to 0.1875
- out_a: bfloat16 [8, 1152, 16], P('seq'), may hold values from -2 to 2
- attn_b: bfloat16 [4, 8, 16, 1152], P(None, 'seq'), may hold values from -1.5 to 1.5
- up_a: bfloat16 [8, 1152, 16], P('seq'), may hold values from -0.1875 to 0.1875
- up_b: bfloat16 [8, 16, 4304], P('seq'), may hold values from -1.5 to 1.5
- down_a: bfloat16 [8, 4304, 16], P('seq'), may hold values from -0.09375 to 0.09375
- down_b: bfloat16 [8, 16, 1152], P('seq'), may hold values from -1.5 to 1.5
Outputs:
- mixed: bfloat16 [32, 1024, 1152], P('dp', 'seq')
- input_grad: float32 [32, 1024, 1152], P('dp', 'seq')
- grad_qkv_a: float32 [3, 8, 1152, 16], P(None, 'seq')
- grad_out_a: float32 [8, 1152, 16], P('seq')
- grad_attn_b: float32 [4, 8, 16, 1152], P(None, 'seq')
- grad_up_a: float32 [8, 1152, 16], P('seq')
- grad_up_b: float32 [8, 16, 4304], P('seq')
- grad_down_a: float32 [8, 4304, 16], P('seq')
- grad_down_b: float32 [8, 16, 1152], P('seq')
Inputs may be any that keep to these rules, and one draw needn't show every extreme that they name: `lengths`: each row lists the patch counts of its pictures in order, each 100 to 1024, then zeros; the counts sum to at most 1024 and the rest of the row is padding. In each aligned group of 2 rows one row holds a single picture of 1024 patches. `adapter_ids`: slots after a row's last picture are unused.
All inputs are finite; a program needn't handle non-finite values.
Results may differ from a plain program's by a relative error of at most 0.019.
Values may be sent and summed in bfloat16 or wider, within the bound.
A program may use at most 320 MiB of HBM per device.

v0:
```python
from functools import partial

import jax
import jax.numpy as jnp
from jax import lax
from jax.sharding import PartitionSpec as P

HEADS = 16
HEAD_DIM = 72
RANK = 16
ADAPTERS = 8


adapter_scale = 0.5
norm_eps = 1e-06
masked_score = -1e30
head_group = 4


def layer_norm(values, gain_vec, shift_vec):
    center = jnp.mean(values, axis=-1, keepdims=True)
    centered = values - center
    variance = jnp.mean(centered * centered, axis=-1, keepdims=True)
    return centered * lax.rsqrt(variance + norm_eps) * gain_vec + shift_vec


def gelu_tanh(values):
    return jax.nn.gelu(values, approximate=True)


def default_product(left_op, right_op):
    return jnp.dot(left_op, right_op, preferred_element_type=jnp.float32)


def reverse_product(left_op, right_op):
    return lax.dot_general(
        left_op, right_op, (((1,), (1,)), ((), ())), preferred_element_type=jnp.float32
    )


def token_product(left_op, right_op):
    return lax.dot_general(
        left_op, right_op, (((0,), (0,)), ((), ())), preferred_element_type=jnp.float32
    )


def flat_down(matrix):
    return jnp.transpose(matrix, (1, 0, 2)).reshape(
        matrix.shape[1], matrix.shape[0] * matrix.shape[2]
    )


def flattened_up_factor(matrix):
    return matrix.reshape(matrix.shape[0] * matrix.shape[1], matrix.shape[2])


def unflat_down(matrix):
    return jnp.transpose(matrix.reshape(matrix.shape[0], ADAPTERS, RANK), (1, 0, 2))


def unflat_up(matrix):
    return matrix.reshape(ADAPTERS, RANK, matrix.shape[1])


def picture_ids(lengths, positions):
    pic_ends = jnp.cumsum(lengths, axis=1, dtype=jnp.int32)
    picture = jnp.sum(
        (positions[None, :, None] >= pic_ends[:, None, :]).astype(jnp.int32),
        axis=2,
        dtype=jnp.int32,
    )
    return (picture, positions[None, :] < pic_ends[:, -1:])


def token_info(lengths, adapter_ids, positions):
    picture, is_live = picture_ids(lengths, positions)
    slot_ids = jnp.arange(lengths.shape[1], dtype=jnp.int32)
    adapter = jnp.sum(
        jnp.where(picture[:, :, None] == slot_ids, adapter_ids[:, None, :], 0),
        axis=2,
        dtype=jnp.int32,
    )
    chosen = (adapter[:, :, None] == jnp.arange(ADAPTERS, dtype=jnp.int32)) & is_live[:, :, None]
    column_mask = jnp.repeat(chosen.astype(jnp.float32), RANK, axis=2)
    return (picture, is_live, column_mask)


def adapter_apply_pass(inputs, column_mask, down_flat, up_factor_flattened):
    hidden_state = (default_product(inputs, down_flat) * column_mask).astype(jnp.bfloat16)
    return (adapter_scale * default_product(hidden_state, up_factor_flattened), hidden_state)


def adapter_grad_pass(
    inputs, hidden_state, column_mask, down_flat, up_factor_flattened, lowrank_gradient
):
    hidden_gradient = (
        adapter_scale * reverse_product(lowrank_gradient, up_factor_flattened) * column_mask
    ).astype(jnp.bfloat16)
    grad_down = token_product(inputs, hidden_gradient)
    upward_gradient = adapter_scale * token_product(hidden_state, lowrank_gradient)
    return (reverse_product(hidden_gradient, down_flat), grad_down, upward_gradient)


def split_heads(rows):
    return jnp.transpose(
        rows.reshape(rows.shape[0], HEADS // head_group, head_group, HEAD_DIM), (1, 0, 2, 3)
    )


def join_heads(groups):
    return jnp.transpose(groups, (1, 0, 2, 3)).reshape(groups.shape[1], HEADS * HEAD_DIM)


def forward_group(packed, allowed):
    q_grp, k_grp, v_grp = packed
    scores = jnp.einsum(
        "qhd,khd->hqk", q_grp, k_grp, preferred_element_type=jnp.float32
    ) * HEAD_DIM ** (-0.5)
    scores = jnp.where(allowed[None], scores, masked_score)
    top_score = jnp.max(scores, axis=-1, keepdims=True)
    weights = jnp.exp(scores - top_score)
    total_sum = jnp.sum(weights, axis=-1, keepdims=True)
    attn_probs = (weights / total_sum).astype(jnp.bfloat16)
    layer_result = jnp.einsum("hqk,khd->qhd", attn_probs, v_grp, preferred_element_type=jnp.float32)
    return (layer_result, top_score[..., 0] + jnp.log(total_sum[..., 0]))


def group_grads(q_grp, k_grp, v_grp, do_grp, lse_grp, allowed):
    scale = HEAD_DIM ** (-0.5)
    scores = jnp.einsum("qhd,khd->hqk", q_grp, k_grp, preferred_element_type=jnp.float32) * scale
    scores = jnp.where(allowed[None], scores, masked_score)
    probs_full = jnp.exp(scores - lse_grp[..., None])
    attn_probs = probs_full.astype(jnp.bfloat16)
    d_prob = jnp.einsum("qhd,khd->hqk", do_grp, v_grp, preferred_element_type=jnp.float32)
    row_delta = jnp.sum(probs_full * d_prob, axis=-1)
    d_score = (probs_full * (d_prob - row_delta[..., None])).astype(jnp.bfloat16)
    d_query = jnp.einsum("hqk,khd->qhd", d_score, k_grp, preferred_element_type=jnp.float32) * scale
    d_key = jnp.einsum("hqk,qhd->khd", d_score, q_grp, preferred_element_type=jnp.float32) * scale
    d_value = jnp.einsum("hqk,qhd->khd", attn_probs, do_grp, preferred_element_type=jnp.float32)
    return (d_query, d_key, d_value, row_delta)


def backward_group(packed, allowed):
    q_grp, k_grp, v_grp, do_grp, lse_grp = packed
    return group_grads(q_grp, k_grp, v_grp, do_grp, lse_grp, allowed)


def attend_row(packed):
    q_row, k_row, v_row, q_pic, k_pic = packed
    allowed = q_pic[:, None] == k_pic[None, :]
    results, log_sums = lax.map(
        partial(forward_group, allowed=allowed),
        (split_heads(q_row), split_heads(k_row), split_heads(v_row)),
    )
    return (join_heads(results), log_sums)


def attend_back_row(packed):
    q_row, k_row, v_row, do_row, lse_row, q_pic, k_pic = packed
    allowed = q_pic[:, None] == k_pic[None, :]
    d_query, d_key, d_value, deltas = lax.map(
        partial(backward_group, allowed=allowed),
        (split_heads(q_row), split_heads(k_row), split_heads(v_row), split_heads(do_row), lse_row),
    )
    return (join_heads(d_query), join_heads(d_key), join_heads(d_value), deltas)


def local(
    tokens,
    cotangent,
    lengths,
    adapter_ids,
    w_query,
    w_key,
    w_value,
    w_out,
    w_up,
    w_down,
    b_query,
    b_value,
    b_out,
    b_up,
    b_down,
    gain_one,
    shift_one,
    gain_two,
    shift_two,
    qkv_a,
    out_a,
    attn_b,
    up_a,
    up_b,
    down_a,
    down_b,
):
    seq_count = lax.axis_size("seq")
    row_count, local_len, model_width = tokens.shape
    full_len = local_len * seq_count
    tok_count = row_count * local_len
    gathered = (
        lax.all_gather(w_query, "seq", axis=1, tiled=True),
        lax.all_gather(w_key, "seq", axis=1, tiled=True),
        lax.all_gather(w_value, "seq", axis=1, tiled=True),
        lax.all_gather(w_out, "seq", axis=1, tiled=True),
        lax.all_gather(w_up, "seq", axis=1, tiled=True),
        lax.all_gather(w_down, "seq", axis=0, tiled=True),
        lax.all_gather(b_query, "seq", axis=0, tiled=True),
        lax.all_gather(b_value, "seq", axis=0, tiled=True),
        lax.all_gather(b_out, "seq", axis=0, tiled=True),
        lax.all_gather(b_up, "seq", axis=0, tiled=True),
        lax.all_gather(b_down, "seq", axis=0, tiled=True),
        lax.all_gather(gain_one, "seq", axis=0, tiled=True),
        lax.all_gather(shift_one, "seq", axis=0, tiled=True),
        lax.all_gather(gain_two, "seq", axis=0, tiled=True),
        lax.all_gather(shift_two, "seq", axis=0, tiled=True),
        lax.all_gather(qkv_a, "seq", axis=1, tiled=True),
        lax.all_gather(out_a, "seq", axis=0, tiled=True),
        lax.all_gather(attn_b, "seq", axis=1, tiled=True),
        lax.all_gather(up_a, "seq", axis=0, tiled=True),
        lax.all_gather(up_b, "seq", axis=0, tiled=True),
        lax.all_gather(down_a, "seq", axis=0, tiled=True),
        lax.all_gather(down_b, "seq", axis=0, tiled=True),
    )
    (
        q_rows,
        k_rows,
        v_rows,
        o_rows,
        up_rows,
        down_rows,
        query_proj_bias,
        value_proj_bias,
        out_proj_bias,
        up_proj_bias,
        down_proj_bias,
        gain_norm_one,
        shift_norm_one,
        gain_norm_two,
        shift_norm_two,
        all_qkv_a,
        all_out_a,
        all_attn_b,
        all_up_a,
        all_up_b,
        all_down_a,
        all_down_b,
    ) = gathered
    weights = (
        lax.all_gather(q_rows, "dp", axis=0, tiled=True),
        lax.all_gather(k_rows, "dp", axis=0, tiled=True),
        lax.all_gather(v_rows, "dp", axis=0, tiled=True),
        lax.all_gather(o_rows, "dp", axis=0, tiled=True),
        lax.all_gather(up_rows, "dp", axis=0, tiled=True),
        lax.all_gather(down_rows, "dp", axis=1, tiled=True),
    )
    (
        complete_query_weight,
        complete_key_weight,
        complete_value_weight,
        complete_out_weight,
        complete_up_weight,
        complete_down_weight,
    ) = weights
    query_down_factor = flat_down(all_qkv_a[0])
    key_down_factor = flat_down(all_qkv_a[1])
    value_down_factor = flat_down(all_qkv_a[2])
    attention_down_factor = flat_down(all_out_a)
    first_down_factor = flat_down(all_up_a)
    second_down_factor = flat_down(all_down_a)
    query_up_factor = flattened_up_factor(all_attn_b[0])
    key_up_factor = flattened_up_factor(all_attn_b[1])
    value_up_factor = flattened_up_factor(all_attn_b[2])
    attention_up_factor = flattened_up_factor(all_attn_b[3])
    first_up_factor = flattened_up_factor(all_up_b)
    second_up_factor = flattened_up_factor(all_down_b)
    own_pos = lax.axis_index("seq") * local_len + jnp.arange(local_len, dtype=jnp.int32)
    q_pic, is_live, column_mask = token_info(lengths, adapter_ids, own_pos)
    k_pic, key_live = picture_ids(lengths, jnp.arange(full_len, dtype=jnp.int32))
    flattened_mask = column_mask.reshape(tok_count, ADAPTERS * RANK)
    live_flat = is_live.reshape(tok_count, 1)
    flattened_input = tokens.reshape(tok_count, model_width).astype(jnp.float32)
    normed, norm_back_one = jax.vjp(
        partial(layer_norm, gain_vec=gain_norm_one, shift_vec=shift_norm_one), flattened_input
    )
    normed_lowrank = normed.astype(jnp.bfloat16)
    query_adapter_term, query_hidden_lowrank = adapter_apply_pass(
        normed_lowrank, flattened_mask, query_down_factor, query_up_factor
    )
    key_adapter_term, key_hidden_lowrank = adapter_apply_pass(
        normed_lowrank, flattened_mask, key_down_factor, key_up_factor
    )
    value_adapter_term, value_hidden_lowrank = adapter_apply_pass(
        normed_lowrank, flattened_mask, value_down_factor, value_up_factor
    )
    query_lowrank = (
        default_product(normed_lowrank, complete_query_weight)
        + query_proj_bias
        + query_adapter_term
    ).astype(jnp.bfloat16)
    key_lowrank = (default_product(normed_lowrank, complete_key_weight) + key_adapter_term).astype(
        jnp.bfloat16
    )
    value_lowrank = (
        default_product(normed_lowrank, complete_value_weight)
        + value_proj_bias
        + value_adapter_term
    ).astype(jnp.bfloat16)
    query_rows = query_lowrank.reshape(row_count, local_len, model_width)
    key_rows = key_lowrank.reshape(row_count, local_len, model_width)
    value_rows = value_lowrank.reshape(row_count, local_len, model_width)
    keys_full, values_full = (
        lax.all_gather(key_rows, "seq", axis=1, tiled=True),
        lax.all_gather(value_rows, "seq", axis=1, tiled=True),
    )
    attended, log_sums = lax.map(attend_row, (query_rows, keys_full, values_full, q_pic, k_pic))
    attention_lowrank = attended.reshape(tok_count, model_width).astype(jnp.bfloat16)
    attention_adapter_term, attention_hidden_lowrank = adapter_apply_pass(
        attention_lowrank, flattened_mask, attention_down_factor, attention_up_factor
    )
    middle_activation = flattened_input + (
        default_product(attention_lowrank, complete_out_weight)
        + out_proj_bias
        + attention_adapter_term
    )
    normed_two, norm_back_two = jax.vjp(
        partial(layer_norm, gain_vec=gain_norm_two, shift_vec=shift_norm_two), middle_activation
    )
    second_normed_lowrank = normed_two.astype(jnp.bfloat16)
    first_adapter_term, first_hidden_lowrank = adapter_apply_pass(
        second_normed_lowrank, flattened_mask, first_down_factor, first_up_factor
    )
    preactivation = (
        default_product(second_normed_lowrank, complete_up_weight)
        + up_proj_bias
        + first_adapter_term
    )
    activated, gelu_back = jax.vjp(gelu_tanh, preactivation)
    activation_lowrank = activated.astype(jnp.bfloat16)
    second_adapter_term, second_hidden_lowrank = adapter_apply_pass(
        activation_lowrank, flattened_mask, second_down_factor, second_up_factor
    )
    layer_result = (
        middle_activation
        + default_product(activation_lowrank, complete_down_weight)
        + down_proj_bias
        + second_adapter_term
    )
    mixed_out = layer_result.astype(jnp.bfloat16).reshape(row_count, local_len, model_width)
    regathered = (
        lax.all_gather(w_query, "seq", axis=1, tiled=True),
        lax.all_gather(w_key, "seq", axis=1, tiled=True),
        lax.all_gather(w_value, "seq", axis=1, tiled=True),
        lax.all_gather(w_out, "seq", axis=1, tiled=True),
        lax.all_gather(w_up, "seq", axis=1, tiled=True),
        lax.all_gather(w_down, "seq", axis=0, tiled=True),
    )
    back_weights = (
        lax.all_gather(regathered[0], "dp", axis=0, tiled=True),
        lax.all_gather(regathered[1], "dp", axis=0, tiled=True),
        lax.all_gather(regathered[2], "dp", axis=0, tiled=True),
        lax.all_gather(regathered[3], "dp", axis=0, tiled=True),
        lax.all_gather(regathered[4], "dp", axis=0, tiled=True),
        lax.all_gather(regathered[5], "dp", axis=1, tiled=True),
    )
    back_query, back_key, back_value, reverse_out_proj, reverse_up_proj, reverse_down_proj = (
        back_weights
    )
    cot_flat = cotangent.reshape(tok_count, model_width)
    output_lowrank_gradient = jnp.where(live_flat, cot_flat, jnp.zeros_like(cot_flat))
    activation_adapter_gradient, second_factor_a_gradient, second_factor_b_gradient = (
        adapter_grad_pass(
            activation_lowrank,
            second_hidden_lowrank,
            flattened_mask,
            second_down_factor,
            second_up_factor,
            output_lowrank_gradient,
        )
    )
    activation_lowrank_gradient = (
        reverse_product(output_lowrank_gradient, reverse_down_proj) + activation_adapter_gradient
    ).astype(jnp.bfloat16)
    preactivation_lowrank_gradient = gelu_back(activation_lowrank_gradient.astype(jnp.float32))[
        0
    ].astype(jnp.bfloat16)
    normed_adapter_gradient, first_factor_a_gradient, first_factor_b_gradient = adapter_grad_pass(
        second_normed_lowrank,
        first_hidden_lowrank,
        flattened_mask,
        first_down_factor,
        first_up_factor,
        preactivation_lowrank_gradient,
    )
    second_normed_gradient = (
        reverse_product(preactivation_lowrank_gradient, reverse_up_proj) + normed_adapter_gradient
    )
    d_middle = (
        output_lowrank_gradient.astype(jnp.float32) + norm_back_two(second_normed_gradient)[0]
    )
    branch_lowrank_gradient = d_middle.astype(jnp.bfloat16)
    attention_adapter_gradient, attention_factor_a_gradient, attention_factor_b_gradient = (
        adapter_grad_pass(
            attention_lowrank,
            attention_hidden_lowrank,
            flattened_mask,
            attention_down_factor,
            attention_up_factor,
            branch_lowrank_gradient,
        )
    )
    attention_lowrank_gradient = (
        reverse_product(branch_lowrank_gradient, reverse_out_proj) + attention_adapter_gradient
    ).astype(jnp.bfloat16)
    do_rows = attention_lowrank_gradient.reshape(row_count, local_len, model_width)
    d_query, d_key_part, d_value_part, unused_delta = lax.map(
        attend_back_row, (query_rows, keys_full, values_full, do_rows, log_sums, q_pic, k_pic)
    )
    d_key_own, d_value_own = (
        lax.psum_scatter(
            d_key_part.astype(jnp.bfloat16), "seq", scatter_dimension=1, tiled=True
        ).astype(jnp.float32),
        lax.psum_scatter(
            d_value_part.astype(jnp.bfloat16), "seq", scatter_dimension=1, tiled=True
        ).astype(jnp.float32),
    )
    dq_low = d_query.reshape(tok_count, model_width).astype(jnp.bfloat16)
    dk_low = d_key_own.reshape(tok_count, model_width).astype(jnp.bfloat16)
    dv_low = d_value_own.reshape(tok_count, model_width).astype(jnp.bfloat16)
    query_adapter_gradient, query_factor_a_gradient, query_factor_b_gradient = adapter_grad_pass(
        normed_lowrank,
        query_hidden_lowrank,
        flattened_mask,
        query_down_factor,
        query_up_factor,
        dq_low,
    )
    key_adapter_gradient, key_factor_a_gradient, key_factor_b_gradient = adapter_grad_pass(
        normed_lowrank, key_hidden_lowrank, flattened_mask, key_down_factor, key_up_factor, dk_low
    )
    value_adapter_gradient, value_factor_a_gradient, value_factor_b_gradient = adapter_grad_pass(
        normed_lowrank,
        value_hidden_lowrank,
        flattened_mask,
        value_down_factor,
        value_up_factor,
        dv_low,
    )
    d_normed = (
        reverse_product(dq_low, back_query)
        + reverse_product(dk_low, back_key)
        + reverse_product(dv_low, back_value)
        + query_adapter_gradient
        + key_adapter_gradient
        + value_adapter_gradient
    )
    d_input = d_middle + norm_back_one(d_normed)[0]
    grad_qkv_a = jnp.stack(
        [
            unflat_down(query_factor_a_gradient),
            unflat_down(key_factor_a_gradient),
            unflat_down(value_factor_a_gradient),
        ]
    )
    grad_out_a = unflat_down(attention_factor_a_gradient)
    grad_attn_b = jnp.stack(
        [
            unflat_up(query_factor_b_gradient),
            unflat_up(key_factor_b_gradient),
            unflat_up(value_factor_b_gradient),
            unflat_up(attention_factor_b_gradient),
        ]
    )
    grad_up_a = unflat_down(first_factor_a_gradient)
    grad_up_b = unflat_up(first_factor_b_gradient)
    grad_down_a = unflat_down(second_factor_a_gradient)
    grad_down_b = unflat_up(second_factor_b_gradient)
    shares = (
        lax.psum_scatter(
            grad_qkv_a.astype(jnp.bfloat16), "seq", scatter_dimension=1, tiled=True
        ).astype(jnp.float32),
        lax.psum_scatter(
            grad_out_a.astype(jnp.bfloat16), "seq", scatter_dimension=0, tiled=True
        ).astype(jnp.float32),
        lax.psum_scatter(
            grad_attn_b.astype(jnp.bfloat16), "seq", scatter_dimension=1, tiled=True
        ).astype(jnp.float32),
        lax.psum_scatter(
            grad_up_a.astype(jnp.bfloat16), "seq", scatter_dimension=0, tiled=True
        ).astype(jnp.float32),
        lax.psum_scatter(
            grad_up_b.astype(jnp.bfloat16), "seq", scatter_dimension=0, tiled=True
        ).astype(jnp.float32),
        lax.psum_scatter(
            grad_down_a.astype(jnp.bfloat16), "seq", scatter_dimension=0, tiled=True
        ).astype(jnp.float32),
        lax.psum_scatter(
            grad_down_b.astype(jnp.bfloat16), "seq", scatter_dimension=0, tiled=True
        ).astype(jnp.float32),
    )
    totals = (
        lax.psum(shares[0].astype(jnp.bfloat16), "dp").astype(jnp.float32),
        lax.psum(shares[1].astype(jnp.bfloat16), "dp").astype(jnp.float32),
        lax.psum(shares[2].astype(jnp.bfloat16), "dp").astype(jnp.float32),
        lax.psum(shares[3].astype(jnp.bfloat16), "dp").astype(jnp.float32),
        lax.psum(shares[4].astype(jnp.bfloat16), "dp").astype(jnp.float32),
        lax.psum(shares[5].astype(jnp.bfloat16), "dp").astype(jnp.float32),
        lax.psum(shares[6].astype(jnp.bfloat16), "dp").astype(jnp.float32),
    )
    return (
        mixed_out,
        d_input.reshape(row_count, local_len, model_width),
        totals[0],
        totals[1],
        totals[2],
        totals[3],
        totals[4],
        totals[5],
        totals[6],
    )


def solution(mesh):
    return jax.shard_map(
        local,
        mesh=mesh,
        in_specs=(
            P("dp", "seq", None),
            P("dp", "seq", None),
            P("dp", None),
            P("dp", None),
            P("dp", "seq"),
            P("dp", "seq"),
            P("dp", "seq"),
            P("dp", "seq"),
            P("dp", "seq"),
            P("seq", "dp"),
            P("seq"),
            P("seq"),
            P("seq"),
            P("seq"),
            P("seq"),
            P("seq"),
            P("seq"),
            P("seq"),
            P("seq"),
            P(None, "seq", None, None),
            P("seq", None, None),
            P(None, "seq", None, None),
            P("seq", None, None),
            P("seq", None, None),
            P("seq", None, None),
            P("seq", None, None),
        ),
        out_specs=(
            P("dp", "seq", None),
            P("dp", "seq", None),
            P(None, "seq", None, None),
            P("seq", None, None),
            P(None, "seq", None, None),
            P("seq", None, None),
            P("seq", None, None),
            P("seq", None, None),
            P("seq", None, None),
        ),
        check_vma=False,
    )
```

profile of v0, /device:TPU:0, one launch (start us, length us, event | category | flops | bytes accessed | tf_op | source)
XLA Modules:
  0.0 1252.2 jit_solution(2977364375396471157)
XLA Ops:
  69.2 14.5 %all-gather.22.cloned.1.call-done = bf16[1152,1152]{1,0:T(8,128)(2,1)} async-done(((bf16[72,1152]{1,0:T(8,128)(2,1)}), bf16[1152,1152]{1,0:T(8,128)(2,1)}) %all-gather.22.cloned.1.call-update) | async-done | bytes 2654224 | tf_op jit(solution)/shard_map/all_gather | solution.py:250
  98.9 29.6 %all-gather.26.cloned.1.call-done = bf16[1152,1152]{1,0:T(8,128)(2,1)} async-done(((bf16[72,1152]{1,0:T(8,128)(2,1)}), bf16[1152,1152]{1,0:T(8,128)(2,1)}) %all-gather.26.cloned.1.call-update) | async-done | bytes 2654224 | tf_op jit(solution)/shard_map/all_gather | solution.py:251
  147.6 11.5 all-gather.4
  205.1 11.7 fusion.128
  225.7 39.7 %all-gather.24.cloned.1.call-done = bf16[2,1024,1152]{1,2,0:T(8,128)(2,1)} async-done(((bf16[2,512,1152]{1,2,0:T(8,128)(2,1)}), bf16[2,1024,1152]{1,2,0:T(8,128)(2,1)}) %all-gather.24.cloned.1.call-update) | async-done | bytes 4718608 | tf_op jit(solution)/shard_map/all_gather | solution.py:312
  265.4 64.8 %all-gather.28.cloned.1.call-done = bf16[2,1024,1152]{1,2,0:T(8,128)(2,1)} async-done(((bf16[2,512,1152]{1,2,0:T(8,128)(2,1)}), bf16[2,1024,1152]{1,2,0:T(8,128)(2,1)}) %all-gather.28.cloned.1.call-update) | async-done | bytes 4718608 | tf_op jit(solution)/shard_map/all_gather | solution.py:313
  331.8 91.6 %while.55 = (s32[]{:T(128)}, bf16[2,512,1152]{2,1,0:T(8,128)(2,1)}, f32[2,4,4,512]{3,2,1,0:T(4,128)}, bf16[2,512,1152]{1,2,0:T(8,128)(2,1)}, bf16[2,1024,1152]{1...) while((s32[]{:T(128)}, bf16[2,512,1152]{2,1,0:T(8,128)(2,1)}, ...), condition=%wide.region_11.12_spmd, body=%wide.region_6.11_spmd.sunk | while | flops 629667840 | bytes 65540616 | solution.py:315
  336.3 37.6 %while.58 = (s32[]{:T(128)}, bf16[4,512,4,72]{1,3,2,0:T(8,128)(2,1)}, f32[4,4,512]{2,1,0:T(4,128)}, bf16[4,1024,4,72]{1,3,2,0:T(8,128)(2,1)}, bf16[4,512,4,72]{1...) while((s32[]{:T(128)}, ...), condition=%wide.region_10.10_spmd.clone, body=%wide.region_7.9_spmd.clone.sunk | while | flops 629667840 | bytes 38838432 | solution.py:151
  382.0 37.6 %while.58 = (s32[]{:T(128)}, bf16[4,512,4,72]{1,3,2,0:T(8,128)(2,1)}, f32[4,4,512]{2,1,0:T(4,128)}, bf16[4,1024,4,72]{1,3,2,0:T(8,128)(2,1)}, bf16[4,512,4,72]{1...) while((s32[]{:T(128)}, ...), condition=%wide.region_10.10_spmd.clone, body=%wide.region_7.9_spmd.clone.sunk | while | flops 629667840 | bytes 38838432 | solution.py:151
  448.5 37.3 %all-gather.32.cloned.1.call-done = bf16[1152,4304]{1,0:T(8,128)(2,1)} async-done(((bf16[72,4304]{1,0:T(8,128)(2,1)}), bf16[1152,4304]{1,0:T(8,128)(2,1)}) %all-gather.32.cloned.1.call-update) | async-done | bytes 9916432 | tf_op jit(solution)/shard_map/all_gather | solution.py:253
  485.8 27.3 %multiply_convert_fusion.1 = (bf16[1024,4304]{0,1:T(8,128)(2,1)}, f32[1024,4304]{0,1:T(8,128)}) fusion(f32[1024,4304]{0,1:T(8,128)} %fusion.127, f32[4304]{0:T(1024)S(1)} %copy-done.94, bf16[1024,1152]{1,0:T(8,128)(2,1)} %copy-done.31, bf16[1152,4304]{1,0:T(8,128)(2,1)} %all-gather.32.cloned.1.call-done), kind=kOutput, calls=%fused_computation.94 | convolution fusion | flops 10207297536 | bytes 56365888 | tf_op jit(solution)/shard_map/dot_general | solution.py:32
  513.1 58.7 %all-gather.36.cloned.1.call-done = bf16[4304,1152]{0,1:T(8,128)(2,1)} async-done(((bf16[4304,72]{0,1:T(8,128)(2,1)}), bf16[4304,1152]{0,1:T(8,128)(2,1)}) %all-gather.36.cloned.1.call-update) | async-done | bytes 9916432 | tf_op jit(solution)/shard_map/all_gather | solution.py:254
  571.8 34.0 %fusion.59 = bf16[1024,4304]{0,1:T(8,128)(2,1)} fusion(f32[1024,4304]{0,1:T(8,128)} %get-tuple-element.450, f32[1024,4304]{0,1:T(8,128)} %fusion.128, bf16[1024,1152]{1,0:T(8,128)(2,1)S(1)} %copy-done.26, bf16[4304,1152]{0,1:T(8,128)(2,1)} %all-gather.36.cloned.1.call-done), kind=kOutput, calls=%fused_computation.85 | convolution fusion | flops 10255777792 | bytes 56348672 | tf_op jit(solution)/shard_map/dot_general | solution.py:36
  615.1 22.5 %multiply_reduce_fusion.2 = (f32[1024]{0:T(1024)S(1)}, f32[1024,1152]{1,0:T(8,128)}) fusion(f32[1024,1152]{1,0:T(8,128)} %copy-done.6, f32[1024]{0:T(1024)S(1)} %broadcast_multiply_fusion, f32[1152]{0:T(1024)S(1)} %copy-done.92, f32[1024,1152]{1,0:T(8,128)} %fusion.129, bf16[1024,4304]{0,1:T(8,128)(2,1)} %fusion.59, ...), kind=kOutput, calls=%fused_computation.125 | convolution fusion | flops 10160307200 | bytes 32899584 | tf_op jit(solution)/shard_map/dot_general | solution.py:36
  653.4 184.6 %while.57 = (s32[]{:T(128)}, bf16[2,512,1152]{2,1,0:T(8,128)(2,1)}, bf16[2,1024,1152]{2,1,0:T(8,128)(2,1)}, bf16[2,1024,1152]{2,1,0:T(8,128)(2,1)}, bf16[2,512,1...) while((s32[]{:T(128)}, bf16[2,512,1152]{2,1,0:T(8,128)(2,1)}, ...), condition=%wide.region_20.21_spmd, body=%wide.region_16.20_spmd.sunk | while | flops 1542371328 | bytes 172768896 | solution.py:415
  664.4 67.2 %while.59 = (s32[]{:T(128)}, bf16[4,512,4,72]{1,3,2,0:T(8,128)(2,1)}, bf16[4,1024,4,72]{1,3,2,0:T(8,128)(2,1)}, bf16[4,1024,4,72]{1,3,2,0:T(8,128)(2,1)}, bf16[4...) while((s32[]{:T(128)}, ...), condition=%wide.region_19.19_spmd.clone, body=%wide.region_17.18_spmd.clone.sunk | while | flops 1542371328 | bytes 113446160 | solution.py:161
  756.4 67.2 %while.59 = (s32[]{:T(128)}, bf16[4,512,4,72]{1,3,2,0:T(8,128)(2,1)}, bf16[4,1024,4,72]{1,3,2,0:T(8,128)(2,1)}, bf16[4,1024,4,72]{1,3,2,0:T(8,128)(2,1)}, bf16[4...) while((s32[]{:T(128)}, ...), condition=%wide.region_19.19_spmd.clone, body=%wide.region_17.18_spmd.clone.sunk | while | flops 1542371328 | bytes 113446160 | solution.py:161
  850.0 46.3 %reduce-scatter.16.cloned.1.call-done = bf16[2,512,1152]{2,1,0:T(8,128)(2,1)} async-done(((bf16[2,1024,1152]{2,1,0:T(8,128)(2,1)}), bf16[2,512,1152]{2,1,0:T(8,128)(2,1)}) %reduce-scatter.16.cloned.1.call-update) | async-done | bytes 2359312 | tf_op jit(solution)/shard_map/reduce_scatter | solution.py:422
  902.5 56.3 %reduce-scatter.14.cloned.1.call-done = bf16[2,512,1152]{2,1,0:T(8,128)(2,1)} async-done(((bf16[2,1024,1152]{2,1,0:T(8,128)(2,1)}), bf16[2,512,1152]{2,1,0:T(8,128)(2,1)}) %reduce-scatter.14.cloned.1.call-update) | async-done | bytes 2359312 | tf_op jit(solution)/shard_map/reduce_scatter | solution.py:419
  1017.3 20.6 %fusion.77 = bf16[1024,1152]{1,0:T(8,128)(2,1)} fusion(f32[1024,1152]{1,0:T(8,128)} %convolution_multiply_fusion.3, f32[1024,1152]{1,0:T(8,128)} %copy-done.6, bf16[1024,4304]{0,1:T(8,128)(2,1)} %get-tuple-element.449, bf16[4304,1152]{0,1:T(8,128)(2,1)} %all-gather.36.cloned.1.call-done, f32[1152]{0:T(1024)S(1)} %convert_element_type.281), kind=kOutput, calls=%fused_computation.132 | convolution fusion | flops 10159128576 | bytes 30532096 | tf_op jit(solution)/shard_map/dot_general | solution.py:32
  1064.2 14.1 %reduce-scatter.26.cloned.1.call-done = bf16[4,16,1152]{2,1,0:T(8,128)(2,1)} async-done(((bf16[8,16,1152]{2,1,0:T(8,128)(2,1)}), bf16[4,16,1152]{2,1,0:T(8,128)(2,1)}) %reduce-scatter.26.cloned.1.call-update) | async-done | bytes 147472 | tf_op jit(solution)/shard_map/reduce_scatter | solution.py:496
  1078.3 23.8 %reduce-scatter.22.cloned.1.call-done = bf16[4,16,4304]{2,1,0:T(8,128)(2,1)} async-done(((bf16[8,16,4304]{2,1,0:T(8,128)(2,1)}), bf16[4,16,4304]{2,1,0:T(8,128)(2,1)}) %reduce-scatter.22.cloned.1.call-update) | async-done | bytes 550928 | tf_op jit(solution)/shard_map/reduce_scatter | solution.py:490
  1102.1 24.0 %reduce-scatter.24.cloned.1.call-done = bf16[4,4304,16]{1,2,0:T(8,128)(2,1)} async-done(((bf16[8,4304,16]{1,2,0:T(8,128)(2,1)}), bf16[4,4304,16]{1,2,0:T(8,128)(2,1)}) %reduce-scatter.24.cloned.1.call-update) | async-done | bytes 550928 | tf_op jit(solution)/shard_map/reduce_scatter | solution.py:493
  1133.0 100.5 %all-reduce.17.cloned.1.call-done = (bf16[3,4,1152,16]{2,3,1,0:T(8,128)(2,1)}, bf16[4,1152,16]{1,2,0:T(8,128)(2,1)}, bf16[4,4,16,1152]{3,2,1,0:T(8,128)(2,1)}, b...) async-done(((bf16[3,4,1152,16]{2,3,1,0:T(8,128)(2,1)}, bf16[4,1152,16]{1,2,0:T(8,128)(2,1)}, ...) | async-done | bytes 2576400 | tf_op jit(solution)/shard_map/psum | solution.py:501
  (700 shorter events, 595.4 us)
Async XLA Ops:
  7.3 59.8 %all-gather.20.cloned.1.call-start = ((), (), s32[]{:S(2)}) async-start(), calls=%async_computation.8 | async-start | bytes 1769472 | tf_op jit(solution)/shard_map/all_gather | solution.py:218
  8.0 75.6 %all-gather.22.cloned.1.call-start = ((), (), s32[]{:S(2)}) async-start(), calls=%async_computation.9 | async-start | bytes 2820096 | tf_op jit(solution)/shard_map/all_gather | solution.py:250
  15.6 112.8 %all-gather.26.cloned.1.call-start = ((), (), s32[]{:S(2)}) async-start(), calls=%async_computation.11 | async-start | bytes 2820096 | tf_op jit(solution)/shard_map/all_gather | solution.py:251
  22.2 182.9 %all-gather.38.cloned.1.call-start = ((), (), s32[]{:S(2)}) async-start(), calls=%async_computation.17 | async-start | bytes 1671168 | tf_op jit(solution)/shard_map/all_gather | solution.py:221
  22.8 194.0 %all-gather.18.cloned.1.call-start = ((), (), s32[]{:S(2)}) async-start(), calls=%async_computation.7 | async-start | bytes 2820096 | tf_op jit(solution)/shard_map/all_gather | solution.py:249
  31.7 233.7 %all-gather.24.cloned.1.call-start = ((), (), s32[]{:S(2)}) async-start(), calls=%async_computation.10 | async-start | bytes 7077888 | tf_op jit(solution)/shard_map/all_gather | solution.py:312
  34.9 168.7 %copy-start.7 = (f32[1024,128]{1,0:T(8,128)}, f32[1024,128]{1,0:T(8,128)S(1)}, u32[]{:S(2)}) copy-start(f32[1024,128]{1,0:T(8,128)S(1)} %copy.127) | copy-start | bytes 1572868
  69.2 152.9 %copy-start.34 = (bf16[1,8,16,1152]{3,2,1,0:T(8,128)(2,1)}, bf16[1,8,16,1152]{3,2,1,0:T(8,128)(2,1)S(1)}, u32[]{:S(2)}) copy-start(bf16[1,8,16,1152]{3,2,1,0:T(8,128)(2,1)S(1)} %get-tuple-element.437) | copy-start | bytes 884740
  96.3 233.9 %all-gather.28.cloned.1.call-start = ((), (), s32[]{:S(2)}) async-start(), calls=%async_computation.12 | async-start | bytes 7077888 | tf_op jit(solution)/shard_map/all_gather | solution.py:313
  137.8 288.3 %all-gather.30.cloned.1.call-start = ((), (), s32[]{:S(2)}) async-start(), calls=%async_computation.13 | async-start | bytes 2820096 | tf_op jit(solution)/shard_map/all_gather | solution.py:252
  146.8 291.3 %all-gather.34.cloned.1.call-start = ((), (), s32[]{:S(2)}) async-start(), calls=%async_computation.15 | async-start | bytes 1671168 | tf_op jit(solution)/shard_map/all_gather | solution.py:220
  147.5 338.3 %all-gather.32.cloned.1.call-start = ((), (), s32[]{:S(2)}) async-start(), calls=%async_computation.14 | async-start | bytes 10653696 | tf_op jit(solution)/shard_map/all_gather | solution.py:253
  160.8 411.0 %all-gather.36.cloned.1.call-start = ((), (), s32[]{:S(2)}) async-start(), calls=%async_computation.16 | async-start | bytes 10653696 | tf_op jit(solution)/shard_map/all_gather | solution.py:254
  175.0 721.3 %reduce-scatter.16.cloned.1.call-start = ((), (), s32[]{:S(2)}) async-start(), calls=%async_computation.19 | async-start | bytes 7077888 | tf_op jit(solution)/shard_map/reduce_scatter | solution.py:422
  448.5 123.3 %copy-start.26 = (bf16[1024,1152]{1,0:T(8,128)(2,1)S(1)}, bf16[1024,1152]{1,0:T(8,128)(2,1)}, u32[]{:S(2)}) copy-start(bf16[1024,1152]{1,0:T(8,128)(2,1)} %bitcast_select_fusion) | copy-start | bytes 7077892
  838.0 120.7 %reduce-scatter.14.cloned.1.call-start = ((), (), s32[]{:S(2)}) async-start(), calls=%async_computation.18 | async-start | bytes 7077888 | tf_op jit(solution)/shard_map/reduce_scatter | solution.py:419
  838.7 216.5 %all-reduce.19.cloned.1.call-start = ((), (), s32[]{:S(2)}) async-start(), calls=%async_computation.26 | async-start | bytes 4128768
  850.0 108.7 %copy-start.44 = (bf16[1,8,16,1152]{3,2,1,0:T(8,128)(2,1)S(1)}, bf16[1,8,16,1152]{3,2,1,0:T(8,128)(2,1)}, u32[]{:S(2)}) copy-start(bf16[1,8,16,1152]{3,2,1,0:T(8,128)(2,1)} %copy-done.43) | copy-start | bytes 884740
  972.7 86.2 %reduce-scatter.18.cloned.1.call-start = ((), (), s32[]{:S(2)}) async-start(), calls=%async_computation.20 | async-start | bytes 442368 | tf_op jit(solution)/shard_map/reduce_scatter | solution.py:481
  976.8 87.4 %reduce-scatter.20.cloned.1.call-start = ((), (), s32[]{:S(2)}) async-start(), calls=%async_computation.21 | async-start | bytes 442368 | tf_op jit(solution)/shard_map/reduce_scatter | solution.py:487
  980.2 98.1 %reduce-scatter.26.cloned.1.call-start = ((), (), s32[]{:S(2)}) async-start(), calls=%async_computation.24 | async-start | bytes 442368 | tf_op jit(solution)/shard_map/reduce_scatter | solution.py:496
  987.8 114.3 %reduce-scatter.22.cloned.1.call-start = ((), (), s32[]{:S(2)}) async-start(), calls=%async_computation.22 | async-start | bytes 1671168 | tf_op jit(solution)/shard_map/reduce_scatter | solution.py:490
  995.8 130.3 %reduce-scatter.24.cloned.1.call-start = ((), (), s32[]{:S(2)}) async-start(), calls=%async_computation.23 | async-start | bytes 1671168 | tf_op jit(solution)/shard_map/reduce_scatter | solution.py:493
  1010.0 223.5 %all-reduce.17.cloned.1.call-start = ((), (), s32[]{:S(2)}) async-start(), calls=%async_computation.25 | async-start | bytes 5177344 | tf_op jit(solution)/shard_map/psum | solution.py:501
  (166 other events, 1395.6 us)
Sparse Core Ops, SparseCore 0:
  9.7 27.4 all-gather.19
  39.9 43.6 all-gather.21
  86.4 42.0 all-gather.25
  129.8 24.1 all-gather.37
  156.6 45.9 all-gather.17
  204.0 61.3 all-gather.23
  267.5 62.6 all-gather.27
  332.3 43.3 all-gather.29
  377.3 20.7 all-gather.33
  400.6 85.0 all-gather.31
  488.5 83.2 all-gather.35
  838.1 58.1 reduce-scatter.15
  898.7 59.9 reduce-scatter.13
  972.8 62.3 all-reduce.18
  1037.9 12.0 reduce-scatter.17
  1052.1 12.0 reduce-scatter.19
  1066.3 12.0 reduce-scatter.25
  1081.0 21.0 reduce-scatter.21
  1105.0 21.0 reduce-scatter.23
  1131.1 102.3 all-reduce.16
where the time goes:
time: 1260 us; the launch traced here: 1250 us
  waiting for transfers between devices  518 us (41%)
  matrix products  391 us (31%)
  local copies, waits for them, and re-layouts  144 us (11%)
  other arithmetic  89.6 us (7%)
  blocking collectives  89.1 us (7%)
  between operations  18 us (1%)
    dot_general x18, matrix products, reverse_product(): lax.dot_general(left_op, right_op, (((1,), (1,)), ((), ())), preferred_el...  114 us
    dot_general x18, matrix products, default_product(): return jnp.dot(left_op, right_op, preferred_element_type=jnp.float32)  107 us
    psum x1, waiting for transfers between devices, local(): lax.psum(shares[0].astype(jnp.bfloat16), 'dp').astype(jnp.float32)  101 us
    all_gather x1, waiting for transfers between devices, local(): lax.all_gather(value_rows, 'seq', axis=1, tiled=True)  64.8 us
    all_gather x1, waiting for transfers between devices, local(): lax.all_gather(down_rows, 'dp', axis=1, tiled=True)  58.7 us
    reduce_scatter x1, waiting for transfers between devices, local(): lax.psum_scatter(d_key_part.astype(jnp.bfloat16), 'seq', scatter_dimensio...  56.3 us
    reduce_scatter x1, waiting for transfers between devices, local(): lax.psum_scatter(d_value_part.astype(jnp.bfloat16), 'seq', scatter_dimens...  46.3 us
    all_gather x1, waiting for transfers between devices, local(): lax.all_gather(key_rows, 'seq', axis=1, tiled=True)  39.7 us
  transfers between devices with their start and end apart: 20, of which 13 were waited for; matrix products, arithmetic and copies ran while one was open for 26% of the time, Pallas kernels for 0%

commit v1 on v0

v1 whole, which is shorter than its diff:
```python
from functools import partial

import jax
import jax.numpy as jnp
from jax import lax
from jax.experimental import pallas as pl
from jax.experimental.pallas import tpu as pltpu
from jax.sharding import PartitionSpec as P

HEADS = 16
HEAD_DIM = 72
RANK = 16
ADAPTERS = 8
LORA = RANK * ADAPTERS
LANES = 128
EPS = 1e-06
SCALE = HEAD_DIM ** (-0.5)
BIG = 1e30
LOG2E = 1.4426950408889634
VMEM = 60 * 1024 * 1024

bf16 = jnp.bfloat16
f32 = jnp.float32


def nn(a, b):
    return jnp.dot(a, b, preferred_element_type=f32)


def nt(a, b):
    return lax.dot_general(a, b, (((1,), (1,)), ((), ())), preferred_element_type=f32)


def tn(a, b):
    return lax.dot_general(a, b, (((0,), (0,)), ((), ())), preferred_element_type=f32)


def up128(n):
    return -(-n // LANES) * LANES


def lane_ids(rows):
    return lax.broadcasted_iota(jnp.int32, (rows, LANES), 1)


def norm_parts(x):
    center = jnp.mean(x, axis=-1, keepdims=True)
    xc = x - center
    r = lax.rsqrt(jnp.mean(xc * xc, axis=-1, keepdims=True) + EPS)
    return xc * r, r


def norm_back(dn, gain, nh, r):
    gh = dn * gain
    a = jnp.mean(gh, axis=-1, keepdims=True)
    b = jnp.mean(gh * nh, axis=-1, keepdims=True)
    return r * (gh - a - nh * b)


def column_mask(aid):
    return (lane_ids(aid.shape[0]) // RANK == aid).astype(f32)


def qkv_kernel(nh, tm, x_ref, w_ref, at_ref, b_ref, bias_ref, vec_ref, aid_ref, pic_ref,
               out_ref, n1_ref, h_ref):
    p = pl.program_id(0)
    j = pl.program_id(1)
    tokens = x_ref.shape[0]
    width = nh * HEAD_DIM

    @pl.when((p == 0) & (j == 0))
    def _():
        def norm_step(i, c):
            rows = pl.ds(i * tm, tm)
            nhat, _ = norm_parts(x_ref[rows, :].astype(f32))
            n1_ref[rows, :] = (nhat * vec_ref[4:5, :] + vec_ref[5:6, :]).astype(bf16)
            return c
        lax.fori_loop(0, tokens // tm, norm_step, 0)

    @pl.when(j == 0)
    def _():
        def hidden_step(i, c):
            rows = pl.ds(i * tm, tm)
            h = nt(n1_ref[rows, :], at_ref[0]) * column_mask(aid_ref[rows, :])
            h_ref[0, rows, :] = h.astype(bf16)
            return c
        lax.fori_loop(0, tokens // tm, hidden_step, 0)

    def step(i, c):
        rows = pl.ds(i * tm, tm)
        y = nn(n1_ref[rows, :], w_ref[0])[:, :width]
        y = y + 0.5 * nn(h_ref[0, rows, :], b_ref[0, 0]) + bias_ref[0, 0]
        slot = lane_ids(tm) - HEAD_DIM
        pic = pic_ref[rows, :]
        same = slot == pic
        in_slots = (slot >= 0) & (slot < 16)
        q_aug = jnp.where(same, 1.0, 0.0)
        k_aug = jnp.where(in_slots & jnp.logical_not(same), -BIG, 0.0)
        v_aug = jnp.where((slot == 0) | (slot == 1), 1.0, 0.0)
        aug = jnp.where(p == 0, q_aug, jnp.where(p == 1, k_aug, v_aug))[:, HEAD_DIM:]
        for h in range(nh):
            head = y[:, h * HEAD_DIM:(h + 1) * HEAD_DIM]
            out_ref[0, h, rows, :HEAD_DIM] = head.astype(bf16)
            out_ref[0, h, rows, HEAD_DIM:] = aug.astype(bf16)
        return c
    lax.fori_loop(0, tokens // tm, step, 0)


def qkv_call(x, wa, at, bq, bias, vec, aid, pic):
    tokens, d = x.shape
    s = wa.shape[0]
    nh = HEADS // s
    slot = wa.shape[2] // 4
    tm = min(256, tokens)
    return pl.pallas_call(
        partial(qkv_kernel, nh, tm),
        grid=(3, s),
        in_specs=[
            pl.BlockSpec((tokens, d), lambda p, j: (0, 0)),
            pl.BlockSpec((1, d, slot), lambda p, j: (j, 0, p)),
            pl.BlockSpec((1, LORA, d), lambda p, j: (p, 0, 0)),
            pl.BlockSpec((1, 1, LORA, nh * HEAD_DIM), lambda p, j: (p, j, 0, 0)),
            pl.BlockSpec((1, 1, 1, nh * HEAD_DIM), lambda p, j: (p, j, 0, 0)),
            pl.BlockSpec(vec.shape, lambda p, j: (0, 0)),
            pl.BlockSpec((tokens, 1), lambda p, j: (0, 0)),
            pl.BlockSpec((tokens, 1), lambda p, j: (0, 0)),
        ],
        out_specs=[
            pl.BlockSpec((1, nh, tokens, LANES), lambda p, j: (p, j, 0, 0)),
            pl.BlockSpec((tokens, d), lambda p, j: (0, 0)),
            pl.BlockSpec((1, tokens, LORA), lambda p, j: (p, 0, 0)),
        ],
        out_shape=[
            jax.ShapeDtypeStruct((3, HEADS, tokens, LANES), bf16),
            jax.ShapeDtypeStruct((tokens, d), bf16),
            jax.ShapeDtypeStruct((3, tokens, LORA), bf16),
        ],
        compiler_params=pltpu.CompilerParams(vmem_limit_bytes=VMEM),
        name="qkv",
    )(x, wa, at, bq, bias, vec, aid, pic)


def attn_fwd_kernel(tq, q_ref, k_ref, v_ref, p_ref, o_ref):
    def step(i, c):
        rows = pl.ds(i * tq, tq)
        s = nt(q_ref[0, 0, rows, :], k_ref[0, 0])
        top = jnp.max(s, axis=-1, keepdims=True)
        p = jnp.exp2((s - top) * (SCALE * LOG2E)).astype(bf16)
        p_ref[0, rows, :] = p
        o = nn(p, v_ref[0, 0])
        inv = 1.0 / o[:, HEAD_DIM:HEAD_DIM + 1]
        one = inv.astype(bf16).astype(f32)
        two = (inv - one).astype(bf16).astype(f32)
        lane = lane_ids(tq)
        tail = jnp.where(lane == HEAD_DIM, one, jnp.where(lane == HEAD_DIM + 1, two, inv - one - two))
        o_ref[0, rows, :] = jnp.where(lane < HEAD_DIM, o * inv, tail).astype(bf16)
        return c
    lax.fori_loop(0, q_ref.shape[2] // tq, step, 0)


def attn_fwd_call(qkv, kv, off):
    tokens, keys = qkv.shape[2], kv.shape[2]
    tq = min(256, tokens)
    return pl.pallas_call(
        partial(attn_fwd_kernel, tq),
        grid=(HEADS,),
        in_specs=[
            pl.BlockSpec((1, 1, tokens, LANES), lambda h: (0, h, 0, 0)),
            pl.BlockSpec((1, 1, keys, LANES), lambda h: (off, h, 0, 0)),
            pl.BlockSpec((1, 1, keys, LANES), lambda h: (off + 1, h, 0, 0)),
        ],
        out_specs=[
            pl.BlockSpec((1, tokens, keys), lambda h: (h, 0, 0)),
            pl.BlockSpec((1, tokens, LANES), lambda h: (h, 0, 0)),
        ],
        out_shape=[
            jax.ShapeDtypeStruct((HEADS, tokens, keys), bf16),
            jax.ShapeDtypeStruct((HEADS, tokens, LANES), bf16),
        ],
        compiler_params=pltpu.CompilerParams(vmem_limit_bytes=VMEM),
        name="attn_fwd",
    )(qkv, kv, kv)


def attn_bwd_kernel(tq, q_ref, k_ref, v_ref, p_ref, do_ref, dq_ref, dk_ref, dv_ref, ds_ref):
    def step(i, c):
        rows = pl.ds(i * tq, tq)
        dp = nt(do_ref[0, rows, :], v_ref[0, 0])
        ds = (p_ref[0, rows, :].astype(f32) * dp).astype(bf16)
        ds_ref[rows, :] = ds
        dq_ref[0, rows, :] = (nn(ds, k_ref[0, 0]) * SCALE).astype(bf16)
        return c
    lax.fori_loop(0, q_ref.shape[2] // tq, step, 0)
    keys = k_ref.shape[2]
    tk = min(256, keys)

    def key_step(i, c):
        cols = pl.ds(i * tk, tk)
        dv_ref[0, cols, :] = tn(p_ref[0, :, cols], do_ref[0]).astype(bf16)
        dk_ref[0, cols, :] = (tn(ds_ref[:, cols], q_ref[0, 0]) * SCALE).astype(bf16)
        return c
    for i in range(keys // tk):
        key_step(i, 0)


def attn_bwd_call(qkv, kv, off, probs, do_aug):
    tokens, keys = qkv.shape[2], kv.shape[2]
    tq = min(256, tokens)
    return pl.pallas_call(
        partial(attn_bwd_kernel, tq),
        grid=(HEADS,),
        in_specs=[
            pl.BlockSpec((1, 1, tokens, LANES), lambda h: (0, h, 0, 0)),
            pl.BlockSpec((1, 1, keys, LANES), lambda h: (off, h, 0, 0)),
            pl.BlockSpec((1, 1, keys, LANES), lambda h: (off + 1, h, 0, 0)),
            pl.BlockSpec((1, tokens, keys), lambda h: (h, 0, 0)),
            pl.BlockSpec((1, tokens, LANES), lambda h: (h, 0, 0)),
        ],
        out_specs=[
            pl.BlockSpec((1, tokens, LANES), lambda h: (h, 0, 0)),
            pl.BlockSpec((1, keys, LANES), lambda h: (h, 0, 0)),
            pl.BlockSpec((1, keys, LANES), lambda h: (h, 0, 0)),
        ],
        out_shape=[
            jax.ShapeDtypeStruct((HEADS, tokens, LANES), bf16),
            jax.ShapeDtypeStruct((HEADS, keys, LANES), bf16),
            jax.ShapeDtypeStruct((HEADS, keys, LANES), bf16),
        ],
        scratch_shapes=[pltpu.VMEM((tokens, keys), bf16)],
        compiler_params=pltpu.CompilerParams(vmem_limit_bytes=VMEM),
        name="attn_bwd",
    )(qkv, kv, kv, probs, do_aug)


def gelu_parts(z):
    c = 0.7978845608028654
    z2 = z * z
    t = jnp.tanh(z * (c + (c * 0.044715) * z2))
    half = 0.5 * (1.0 + t)
    g = z * half
    dg = half + 0.5 * z * (1.0 - t * t) * (c + (3 * c * 0.044715) * z2)
    return g, dg


def ff_pieces(s, width):
    parts = max(width // 1024, 1)
    step = width // parts // LANES * LANES
    cuts = [k * step for k in range(parts)] + [width]
    return [(j, slice(a, b)) for j in range(s) for a, b in zip(cuts, cuts[1:])]


def mid_kernel(s, slot, oaug_ref, x_ref, cot_ref, aid_ref, wa_ref, wu_ref, wd_ref,
               at_ref, b_ref, ff_ref, bup_ref, vec_ref,
               mixed_ref, dmid_ref, do_ref, go_ref, gff_ref,
               wo_ref, ocat_ref, do_scr, g_ref, dgelu_ref):
    i = pl.program_id(0)
    tm, d = x_ref.shape
    ds = d // s
    pieces = ff_pieces(s, wu_ref.shape[2])
    mask = column_mask(aid_ref[...])
    live = aid_ref[...] >= 0
    bo, bd, gain2, shift2 = vec_ref[2:3, :], vec_ref[3:4, :], vec_ref[6:7, :], vec_ref[7:8, :]
    at_o, at_u, b_o, b_d = at_ref[3], at_ref[4], b_ref[3], b_ref[4]

    @pl.when(i == 0)
    def _():
        for j in range(s):
            wo_ref[:, j * ds:(j + 1) * ds] = wa_ref[j][:, :ds]
        go_ref[...] = jnp.zeros_like(go_ref)
        gff_ref[...] = jnp.zeros_like(gff_ref)

    for h in range(HEADS):
        ocat_ref[:, h * HEAD_DIM:(h + 1) * HEAD_DIM] = oaug_ref[h, :, :HEAD_DIM]
    ocat = ocat_ref[...]
    h_o = (nt(ocat, at_o) * mask).astype(bf16)
    mid = x_ref[...].astype(f32) + nn(ocat, wo_ref[...]) + 0.5 * nn(h_o, b_o) + bo
    nh2, r2 = norm_parts(mid)
    n2 = (nh2 * gain2 + shift2).astype(bf16)
    h_u = (nt(n2, at_u) * mask).astype(bf16)
    h_d = jnp.zeros((tm, LORA), f32)
    out = mid + bd
    for j, cols in pieces:
        z = nn(n2, wu_ref[j, :, cols]) + 0.5 * nn(h_u, ff_ref[1, j, :, cols]) + bup_ref[j, :, cols]
        g, dgelu = gelu_parts(z)
        g = g.astype(bf16)
        g_ref[j, :, cols] = g
        dgelu_ref[j, :, cols] = dgelu.astype(bf16)
        h_d = h_d + nt(g, ff_ref[0, j, :, cols])
        out = out + nt(g, wd_ref[j, :, cols])
    h_d = (h_d * mask).astype(bf16)
    mixed_ref[...] = (out + 0.5 * nn(h_d, b_d)).astype(bf16)

    dy = jnp.where(live, cot_ref[...], jnp.zeros_like(cot_ref))
    dh_d = (0.5 * nt(dy, b_d) * mask).astype(bf16)
    dh_u = jnp.zeros((tm, LORA), f32)
    dn2 = jnp.zeros((tm, d), f32)
    for j, cols in pieces:
        dg = (nn(dy, wd_ref[j, :, cols]) + nn(dh_d, ff_ref[0, j, :, cols])).astype(bf16)
        dz = (dg.astype(f32) * dgelu_ref[j, :, cols].astype(f32)).astype(bf16)
        dh_u = dh_u + nt(dz, ff_ref[1, j, :, cols])
        dn2 = dn2 + nt(dz, wu_ref[j, :, cols])
        gff_ref[0, j, :, cols] += tn(dh_d, g_ref[j, :, cols])
        gff_ref[1, j, :, cols] += 0.5 * tn(h_u, dz)
    dh_u = (0.5 * dh_u * mask).astype(bf16)
    dn2 = dn2 + nn(dh_u, at_u)
    dmid = dy.astype(f32) + norm_back(dn2, gain2, nh2, r2)
    dmid_ref[...] = dmid
    db = dmid.astype(bf16)
    dh_o = (0.5 * nt(db, b_o) * mask).astype(bf16)
    do_scr[...] = (nt(db, wo_ref[...]) + nn(dh_o, at_o)).astype(bf16)
    go_ref[0] += tn(dh_o, ocat)
    go_ref[1] += 0.5 * tn(h_o, db)
    go_ref[2] += tn(dh_u, n2)
    go_ref[3] += 0.5 * tn(h_d, dy)
    lane = lane_ids(tm)[:, HEAD_DIM:]
    for h in range(HEADS):
        parts = oaug_ref[h].astype(f32)
        inv = sum(parts[:, HEAD_DIM + k:HEAD_DIM + k + 1] for k in range(3))
        sl = slice(h * HEAD_DIM, (h + 1) * HEAD_DIM)
        dh = (do_scr[:, sl].astype(f32) * inv).astype(bf16)
        delta = jnp.sum(dh.astype(f32) * ocat_ref[:, sl].astype(f32), axis=-1, keepdims=True)
        hi = delta.astype(bf16).astype(f32)
        lo = delta - hi
        tail = jnp.where(lane == HEAD_DIM, -hi, jnp.where(lane == HEAD_DIM + 1, -lo, 0.0))
        do_ref[h, :, :HEAD_DIM] = dh
        do_ref[h, :, HEAD_DIM:] = tail.astype(bf16)


def mid_call(oaug, x, cot, aid, wa, wu, wd, at, b, ff, bup, vec):
    tokens, d = x.shape
    s = wa.shape[0]
    slot = wa.shape[2] // 4
    fs = wu.shape[2]
    tm = min(256, tokens)
    full = pl.BlockSpec(memory_space=pltpu.VMEM)
    tile = pl.BlockSpec((tm, d), lambda i: (i, 0))
    return pl.pallas_call(
        partial(mid_kernel, s, slot),
        grid=(tokens // tm,),
        in_specs=[
            pl.BlockSpec((HEADS, tm, LANES), lambda i: (0, i, 0)),
            tile, tile,
            pl.BlockSpec((tm, 1), lambda i: (i, 0)),
            pl.BlockSpec((s, d, slot), lambda i: (0, 0, 3), pipeline_mode=pl.Buffered(1)),
            full, full, full, full, full, full, full,
        ],
        out_specs=[
            tile, tile,
            pl.BlockSpec((HEADS, tm, LANES), lambda i: (0, i, 0)),
            full, full,
        ],
        out_shape=[
            jax.ShapeDtypeStruct((tokens, d), bf16),
            jax.ShapeDtypeStruct((tokens, d), f32),
            jax.ShapeDtypeStruct((HEADS, tokens, LANES), bf16),
            jax.ShapeDtypeStruct((4, LORA, d), f32),
            jax.ShapeDtypeStruct((2, s, LORA, fs), f32),
        ],
        scratch_shapes=[
            pltpu.VMEM((d, d), bf16),
            pltpu.VMEM((tm, d), bf16),
            pltpu.VMEM((tm, d), bf16),
            pltpu.VMEM((s, tm, fs), bf16),
            pltpu.VMEM((s, tm, fs), bf16),
        ],
        compiler_params=pltpu.CompilerParams(vmem_limit_bytes=VMEM),
        name="mid",
    )(oaug, x, cot, aid, wa, wu, wd, at, b, ff, bup, vec)


def tail_kernel(s, slot, dq_ref, dk_ref, dv_ref, x_ref, n1_ref, h_ref, dmid_ref, aid_ref,
                w_ref, at_ref, b_ref, vec_ref, out_ref, ga_ref, gb_ref, dy_ref):
    i = pl.program_id(0)
    tm, d = x_ref.shape
    nh = HEADS // s
    ds = d // s
    mask = column_mask(aid_ref[...])

    @pl.when(i == 0)
    def _():
        ga_ref[...] = jnp.zeros_like(ga_ref)
        gb_ref[...] = jnp.zeros_like(gb_ref)

    n1 = n1_ref[...]
    dn = jnp.zeros((tm, d), f32)
    for p, src in enumerate((dq_ref, dk_ref, dv_ref)):
        dh = jnp.zeros((tm, LORA), f32)
        for j in range(s):
            for h in range(nh):
                dy_ref[p, j, :, h * HEAD_DIM:(h + 1) * HEAD_DIM] = src[j * nh + h, :, :HEAD_DIM]
            dy = dy_ref[p, j]
            dh = dh + nt(dy, b_ref[p, j])
            dn = dn + nt(dy, w_ref[j, :, p * slot:p * slot + ds])
            gb_ref[p, j] += 0.5 * tn(h_ref[p], dy)
        dh = (0.5 * dh * mask).astype(bf16)
        dn = dn + nn(dh, at_ref[p])
        ga_ref[p] += tn(dh, n1)
    nhat, r = norm_parts(x_ref[...].astype(f32))
    out_ref[...] = dmid_ref[...] + norm_back(dn, vec_ref[4:5, :], nhat, r)


def tail_call(dq, dk, dv, x, n1, hid, dmid, aid, wa, at, bq, vec):
    tokens, d = x.shape
    s = wa.shape[0]
    slot = wa.shape[2] // 4
    tm = min(256, tokens)
    full = pl.BlockSpec(memory_space=pltpu.VMEM)
    tile = pl.BlockSpec((tm, d), lambda i: (i, 0))
    heads = pl.BlockSpec((HEADS, tm, LANES), lambda i: (0, i, 0))
    return pl.pallas_call(
        partial(tail_kernel, s, slot),
        grid=(tokens // tm,),
        in_specs=[
            heads, heads, heads, tile, tile,
            pl.BlockSpec((3, tm, LORA), lambda i: (0, i, 0)),
            tile,
            pl.BlockSpec((tm, 1), lambda i: (i, 0)),
            full, full, full, full,
        ],
        out_specs=[tile, full, full],
        out_shape=[
            jax.ShapeDtypeStruct((tokens, d), f32),
            jax.ShapeDtypeStruct((3, LORA, d), f32),
            jax.ShapeDtypeStruct((3, s, LORA, d // s), f32),
        ],
        scratch_shapes=[pltpu.VMEM((3, s, tm, d // s), bf16)],
        compiler_params=pltpu.CompilerParams(vmem_limit_bytes=VMEM),
        name="tail",
    )(dq, dk, dv, x, n1, hid, dmid, aid, wa, at, bq, vec)


def rows_of_adapters(a):
    t = jnp.swapaxes(a, -1, -2)
    return t.reshape(*t.shape[:-3], t.shape[-3] * t.shape[-2], t.shape[-1])


def local(tokens, cotangent, lengths, adapter_ids, w_query, w_key, w_value, w_out, w_up, w_down,
          b_query, b_value, b_out, b_up, b_down, gain_one, shift_one, gain_two, shift_two,
          qkv_a, out_a, attn_b, up_a, up_b, down_a, down_b):
    seq = lax.axis_size("seq")
    rows, part_len, d = tokens.shape
    group = seq // rows
    count = rows * part_len
    ds, fs = w_query.shape[1], w_up.shape[1]
    me = lax.axis_index("seq")
    row, chunk = me // group, me % group

    def moves(j):
        return [(a, (a % rows + j) % rows * group + a // rows) for a in range(seq)]

    def send(piece, pairs):
        return piece if all(a == b for a, b in pairs) else lax.ppermute(piece, "seq", pairs)

    def to_row(t):
        out = jnp.zeros((rows, part_len, d), t.dtype)
        for j in range(rows):
            piece = lax.dynamic_index_in_dim(t, (me + j) % rows, 0, False)
            out = lax.dynamic_update_index_in_dim(out, send(piece, moves(j)), (row - j) % rows, 0)
        return out.reshape(count, d)

    def from_row(t, dtype):
        t = t.reshape(rows, part_len, d)
        out = jnp.zeros((rows, part_len, d), dtype)
        for j in range(rows):
            piece = lax.dynamic_index_in_dim(t, (row - j) % rows, 0, False)
            pairs = [(b, a) for a, b in moves(j)]
            if not all(a == b for a, b in pairs):
                piece = piece.astype(bf16)
            got = send(piece, pairs).astype(dtype)
            out = lax.dynamic_update_index_in_dim(out, got, (me + j) % rows, 0)
        return out

    def gather_all(shard):
        full = lax.all_gather(shard, ("seq", "dp"), axis=0, tiled=True)
        return full.reshape(seq, d, shard.shape[1])

    slot = up128(ds)
    pad = ((0, 0), (0, slot - ds))
    wa = gather_all(jnp.concatenate([jnp.pad(w, pad) for w in (w_query, w_key, w_value, w_out)], axis=1))
    wu = gather_all(w_up)
    wd = gather_all(w_down.T)

    vec = jnp.stack([b_query, b_value, b_out, b_down, gain_one, shift_one, gain_two, shift_two])
    vec = lax.all_gather(vec, "seq", axis=1, tiled=True).astype(f32)
    bup = lax.all_gather(b_up[None], "seq", axis=0, tiled=True).astype(f32)[:, None]

    narrow = jnp.concatenate([
        rows_of_adapters(qkv_a), rows_of_adapters(out_a)[None], rows_of_adapters(up_a)[None],
        attn_b.reshape(4, -1, d), down_b.reshape(1, -1, d)])
    wide = jnp.stack([rows_of_adapters(down_a), up_b.reshape(-1, up_b.shape[-1])])
    narrow = lax.all_gather(narrow, "seq", axis=1, tiled=True)
    wide = lax.all_gather(wide, "seq", axis=1, tiled=True)
    at, b = narrow[:5], narrow[5:]
    bq = jnp.swapaxes(b[:3].reshape(3, LORA, seq, ds), 1, 2)
    ff = jnp.swapaxes(wide.reshape(2, LORA, seq, fs), 1, 2)

    my_len = lax.dynamic_index_in_dim(lengths, row, 0, False)
    my_ids = lax.dynamic_index_in_dim(adapter_ids, row, 0, False)
    slots = jnp.arange(my_len.shape[0], dtype=jnp.int32)
    ends = jnp.sum(jnp.where(slots[None, :] <= slots[:, None], my_len[None, :], 0), axis=1)
    pos = chunk * count + jnp.arange(count, dtype=jnp.int32)
    pic = jnp.sum((pos[:, None] >= ends[None, :]).astype(jnp.int32), axis=1, keepdims=True)
    aid = jnp.sum(jnp.where(pic == slots[None, :], my_ids[None, :], 0), axis=1, keepdims=True)
    aid = jnp.where(pos[:, None] < ends[-1], aid, -1)

    x = to_row(tokens)
    cot = to_row(cotangent)
    bias = jnp.stack([vec[0], jnp.zeros_like(vec[0]), vec[1]]).reshape(3, seq, 1, ds)
    qkv, n1, hid = qkv_call(x, wa, at, bq, bias, vec, aid, pic)
    teams = [[g * group + c for c in range(group)] for g in range(rows)]
    if group == 1:
        kv, off = qkv, 1
    else:
        kv = lax.all_gather(qkv[1:], "seq", axis=2, tiled=True, axis_index_groups=teams)
        off = 0
    probs, oaug = attn_fwd_call(qkv, kv, off)
    mixed, dmid, do_aug, g_out, g_ff = mid_call(oaug, x, cot, aid, wa, wu, wd, at, b, ff, bup, vec)
    dq, dk, dv = attn_bwd_call(qkv, kv, off, probs, do_aug)
    if group > 1:
        dk, dv = (lax.psum_scatter(t, "seq", scatter_dimension=1, axis_index_groups=teams, tiled=True)
                  for t in (dk, dv))
    d_in, g_a, g_b = tail_call(dq, dk, dv, x, n1, hid, dmid, aid, wa, at, bq, vec)

    mixed = from_row(mixed, bf16)
    d_in = from_row(d_in, f32)

    def total(t):
        t = lax.psum_scatter(t.astype(bf16), "seq", scatter_dimension=t.ndim - 2, tiled=True)
        return lax.psum(t, "dp").astype(f32)

    g_out, g_ff = total(g_out), total(g_ff)
    g_b = jnp.swapaxes(g_b, 1, 2).reshape(3, LORA, d)
    g_qkv = total(jnp.concatenate([g_a, g_b]))
    g_ff = jnp.swapaxes(g_ff, 1, 2)

    def down_form(t):
        t = t.reshape(*t.shape[:-2], -1, RANK, t.shape[-1])
        return jnp.swapaxes(t, -1, -2)

    def up_form(t):
        return t.reshape(*t.shape[:-2], -1, RANK, t.shape[-1])

    ff_rows = g_ff.reshape(2, -1, seq * fs)
    return (
        mixed,
        d_in,
        down_form(g_qkv[:3]),
        down_form(g_out[0]),
        up_form(jnp.concatenate([g_qkv[3:], g_out[1:2]])),
        down_form(g_out[2]),
        up_form(ff_rows[1]),
        down_form(ff_rows[0]),
        up_form(g_out[3]),
    )


def solution(mesh):
    both = P("dp", "seq", None)
    lead = P("seq", None, None)
    second = P(None, "seq", None, None)
    return jax.shard_map(
        local,
        mesh=mesh,
        in_specs=(both, both, P("dp", None), P("dp", None))
        + (P("dp", "seq"),) * 5 + (P("seq", "dp"),) + (P("seq"),) * 9
        + (second, lead, second, lead, lead, lead, lead),
        out_specs=(both, both, second, lead, second, lead, lead, lead, lead),
        check_vma=False,
    )
```

time: 1260 us -> 852 us (0.68)
  matrix products: 391 us -> 0 us
  Pallas kernels: 0 us -> 298 us
  waiting for transfers between devices: 518 us -> 359 us
  local copies, waits for them, and re-layouts: 144 us -> 55.7 us
  other arithmetic: 89.6 us -> 20.2 us
    dot_general x104 -> x0, matrix products: 391 us -> none  [the longest x18 114 us: reverse_product(): lax.dot_general(left_op, right_op, (((1,), (1,)), ((), ())), preferred_el...]
    pallas_call x0 -> x5, Pallas kernels: none -> 298 us  [the longest x1 131 us: mid_call(): pl.pallas_call(partial(mid_kernel, s, slot), grid=(tokens // tm,), in_spe...]
    reduce_scatter x7 -> x3, waiting for transfers between devices: 170 us -> 89.7 us  [total(): lax.psum_scatter(t.astype(bf16), 'seq', scatter_dimension=t.ndim - 2, til...]
    all_gather x11 -> x5, waiting for transfers between devices: 245 us -> 172 us  [the longest x3 172 us: gather_all(): full = lax.all_gather(shard, ('seq', 'dp'), axis=0, tiled=True)]
    convert_element_type x29 -> x2, other arithmetic: 38.4 us -> 6.68 us  [total(): t.astype(bf16)]
    dynamic_slice x22 -> x0, local copies, waits for them, and re-layouts: 28.3 us -> none  [local(): lax.map(attend_row, (query_rows, keys_full, values_full, q_pic, k_pic))]
    reduce_sum x16 -> x3, other arithmetic: 27.7 us -> 0.29 us  [the longest x1 0.12 us: local(): jnp.sum(jnp.where(slots[None, :] <= slots[:, None], my_len[None, :], 0),...]
    dynamic_update_slice x16 -> x4, local copies, waits for them, and re-layouts: 34.2 us -> 9.04 us  [the longest x2 4.71 us: to_row(): lax.dynamic_update_index_in_dim(out, send(piece, moves(j)), (row - j) % r...]
  transfers between devices with their start and end apart: 20 -> 13, of which waited for: 13 -> 6; matrix products, arithmetic and copies ran while one was open for 26% -> 7% of each run, Pallas kernels for 0% -> 20%
where the time goes in v1:
time: 852 us; the launch traced here: 846 us
  waiting for transfers between devices  359 us (42%)
  Pallas kernels  298 us (35%)
  blocking collectives  91.3 us (11%)
  local copies, waits for them, and re-layouts  55.7 us (7%)
  other arithmetic  20.2 us (2%)
  between operations  15.3 us (2%)
    all_gather x3, waiting for transfers between devices, gather_all(): full = lax.all_gather(shard, ('seq', 'dp'), axis=0, tiled=True)  172 us
    pallas_call x1, Pallas kernels, mid_call(): pl.pallas_call(partial(mid_kernel, s, slot), grid=(tokens // tm,), in_spe...  131 us
    psum x1, waiting for transfers between devices, total(): return lax.psum(t, 'dp').astype(f32)  95.8 us
    reduce_scatter x3, waiting for transfers between devices, total(): lax.psum_scatter(t.astype(bf16), 'seq', scatter_dimension=t.ndim - 2, til...  89.7 us
    all_gather x1, blocking collectives, local(): vec = lax.all_gather(vec, 'seq', axis=1, tiled=True).astype(f32)  82 us
    pallas_call x1, Pallas kernels, attn_bwd_call(): pl.pallas_call(partial(attn_bwd_kernel, tq), grid=(HEADS,), in_specs=[pl....  53 us
    pallas_call x1, Pallas kernels, attn_fwd_call(): pl.pallas_call(partial(attn_fwd_kernel, tq), grid=(HEADS,), in_specs=[pl....  47.6 us
    pallas_call x1, Pallas kernels, qkv_call(): pl.pallas_call(partial(qkv_kernel, nh, tm), grid=(3, s), in_specs=[pl.Blo...  33.9 us
  transfers between devices with their start and end apart: 13, of which 6 were waited for; matrix products, arithmetic and copies ran while one was open for 7% of the time, Pallas kernels for 20%

profile of v1, /device:TPU:0, one launch (start us, length us, event | category | flops | bytes accessed | tf_op | source)
XLA Modules:
  0.0 845.7 jit_solution(2832344804344256863)
XLA Ops:
  14.2 2.8 dynamic-slice_bitcast_fusion.2
  17.1 2.9 collective-permute-start
  26.9 82.0 %all-gather.1 = bf16[2,576,8]{1,2,0:T(8,128)(2,1)S(1)} all-gather(bf16[1,576,8]{1,2,0:T(8,128)(2,1)S(1)} %bitcast.113), channel_id=1, replica_groups=mesh['dp'=16,'seq'=2] {'seq'}, dimensions={0}, use_global_device_ids=true | all-gather | bytes 27648 | tf_op jit(solution)/shard_map/all_gather | solution.py:484
  111.4 9.4 %all-reduce.4 = bf16[4304]{0:T(1024)(128)(2,1)S(1)} all-reduce(bf16[4304]{0:T(1024)(128)(2,1)S(1)} %dynamic-update-slice), channel_id=2, replica_groups=mesh['dp'=16,'seq'=2] {'seq'}, use_global_device_ids=true, to_apply=%add.4 | all-reduce | flops 4304 | bytes 17216
  124.5 3.3 bitcast_dynamic-update-slice_fusion.1
  127.8 4.1 copy.79
  131.9 4.2 copy.80
  139.5 3.8 fusion.13
  143.3 81.7 %all-gather.8.cloned.1.call-done = bf16[2304,2560]{1,0:T(8,128)(2,1)} async-done(((bf16[72,2560]{1,0:T(8,128)(2,1)}), bf16[2304,2560]{1,0:T(8,128)(2,1)}) %all-gather.8.cloned.1.call-update) | async-done | bytes 11796496 | tf_op jit(solution)/shard_map/all_gather | solution.py:474
  225.0 33.9 %qkv.1 = (bf16[3,16,1024,128]{3,2,1,0:T(8,128)(2,1)}, bf16[1024,1152]{1,0:T(8,128)(2,1)}, bf16[3,1024,128]{2,1,0:T(8,128)(2,1)}) custom-call(bf16[1024,1152]{1,0:T(8,128)(2,1)} %bitcast.80, bf16[2,1152,2560]{2,1,0:T(8,128)(2,1)} %bitcast.77, bf16[5,128,1152]{2,1,0:T(8,128)(2,1)} %get-tuple-element.45.at_ref, bf16[3,2,128,576]{3,2,1,0:T(8,128)(2,1)} %bitcast.86, ...), custom_call_target="tpu_custom_call" | custom-call | tf_op jit(solution)/shard_map/qkv/pallas_call | solution.py:115
  258.9 47.6 %attn_fwd.1 = (bf16[16,1024,1024]{2,1,0:T(8,128)(2,1)}, bf16[16,1024,128]{2,1,0:T(8,128)(2,1)}) custom-call(bf16[3,16,1024,128]{3,2,1,0:T(8,128)(2,1)} %get-tuple-element.25.q_ref.k_ref.v_ref, bf16[3,16,1024,128]{3,2,1,0:T(8,128)(2,1)} %get-tuple-element.25.q_ref.k_ref.v_ref, bf16[3,16,1024,128]{3,2,1,0:T(8,128)(2,1)} %get-tuple-element.25.q_ref.k_ref.v_ref), custom_call_target="tpu_custom_call" | custom-call | tf_op jit(solution)/shard_map/attn_fwd/pallas_call | solution.py:164
  306.6 4.4 all-gather.12.cloned.1.call-done
  311.0 85.8 %all-gather.14.cloned.1.call-done = bf16[2304,2152]{1,0:T(8,128)(2,1)} async-done(((bf16[72,2152]{1,0:T(8,128)(2,1)}), bf16[2304,2152]{1,0:T(8,128)(2,1)}) %all-gather.14.cloned.1.call-update) | async-done | bytes 9916432 | tf_op jit(solution)/shard_map/all_gather | solution.py:474
  396.8 130.9 %mid.1 = (bf16[1024,1152]{1,0:T(8,128)(2,1)}, f32[1024,1152]{1,0:T(8,128)}, bf16[16,1024,128]{2,1,0:T(8,128)(2,1)}, f32[4,128,1152]{2,1,0:T(8,128)}, f32[2,2,128,2152]{3,2,1,0:T(8,128)}) custom-call(bf16[16,1024,128]{2,1,0:T(8,128)(2,1)} %get-tuple-element.26.oaug_ref, bf16[1024,1152]{1,0:T(8,128)(2,1)} %bitcast.81, bf16[1024,1152]{1,0:T(8,128)(2,1)} %bitcast.24.cot_ref, ...), custom_call_target="tpu_custom_call" | custom-call | tf_op jit(solution)/shard_map/mid/pallas_call | solution.py:337
  527.7 2.8 convert_element_type.38
  530.6 53.0 %attn_bwd.1 = (bf16[16,1024,128]{2,1,0:T(8,128)(2,1)}, bf16[16,1024,128]{2,1,0:T(8,128)(2,1)}, bf16[16,1024,128]{2,1,0:T(8,128)(2,1)}) custom-call(bf16[3,16,1024,128]{3,2,1,0:T(8,128)(2,1)} %get-tuple-element.25.q_ref.k_ref.v_ref, bf16[3,16,1024,128]{3,2,1,0:T(8,128)(2,1)} %get-tuple-element.25.q_ref.k_ref.v_ref, ...), custom_call_target="tpu_custom_call" | custom-call | tf_op jit(solution)/shard_map/attn_bwd/pallas_call | solution.py:209
  583.6 32.2 %tail.1 = (f32[1024,1152]{1,0:T(8,128)}, f32[3,128,1152]{2,1,0:T(8,128)}, f32[3,2,128,576]{3,2,1,0:T(8,128)}) custom-call(bf16[16,1024,128]{2,1,0:T(8,128)(2,1)} %get-tuple-element.30.dq_ref, bf16[16,1024,128]{2,1,0:T(8,128)(2,1)} %get-tuple-element.31.dk_ref, bf16[16,1024,128]{2,1,0:T(8,128)(2,1)} %get-tuple-element.32.dv_ref, bf16[1024,1152]{1,0:T(8,128)(2,1)} %bitcast.82, ...), custom_call_target="tpu_custom_call" | custom-call | tf_op jit(solution)/shard_map/tail/pallas_call | solution.py:410
  622.1 3.9 convert_element_type.40
  633.9 30.0 %reduce-scatter.4.cloned.1.call-done = bf16[6,64,1152]{2,1,0:T(8,128)(2,1)} async-done(((bf16[6,128,1152]{2,1,0:T(8,128)(2,1)}), bf16[6,64,1152]{2,1,0:T(8,128)(2,1)}) %reduce-scatter.4.cloned.1.call-update) | async-done | bytes 884752 | tf_op jit(solution)/shard_map/reduce_scatter | solution.py:528
  663.9 59.7 %reduce-scatter.8.cloned.1.call-done = bf16[2,2,64,2152]{3,2,1,0:T(8,128)(2,1)} async-done(((bf16[2,2,128,2152]{3,2,1,0:T(8,128)(2,1)}), bf16[2,2,64,2152]{3,2,1,0:T(8,128)(2,1)}) %reduce-scatter.8.cloned.1.call-update) | async-done | bytes 1101840 | tf_op jit(solution)/shard_map/reduce_scatter | solution.py:528
  723.6 2.5 broadcast_in_dim.90
  726.1 3.2 dynamic-slice_dynamic-update-slice_fusion
  730.4 2.8 convert_dynamic-update-slice_fusion
  733.3 95.8 %all-reduce.8.cloned.1.call-done = (bf16[6,64,1152]{2,1,0:T(8,128)(2,1)}, bf16[4,64,1152]{2,1,0:T(8,128)(2,1)}, bf16[2,64,2,2152]{3,1,2,0:T(8,128)(2,1)}) async-done(((bf16[6,64,1152]{2,1,0:T(8,128)(2,1)}, bf16[4,64,1152]{2,1,0:T(8,128)(2,1)}, bf16[2,64,2,2152]{3,1,2,0:T(8,128)(2,1)}), (bf16[6,64,1152]{2,1,0:T(8,128)(2,1)}, bf16[4,64,1152]{2,1,0:T(8,128)(2,1)}, ...) | async-done | bytes 2576400 | tf_op jit(solution)/shard_map/psum | solution.py:529
  (143 shorter events, 47.5 us)
Async XLA Ops:
  7.2 120.6 %all-gather.16.cloned.1.call-start = ((), (), s32[]{:S(2)}) async-start(), calls=%async_computation.7 | async-start | bytes 3342336 | tf_op jit(solution)/shard_map/all_gather | solution.py:492
  9.7 126.4 %all-gather.10.cloned.1.call-start = ((), (), s32[]{:S(2)}) async-start(), calls=%async_computation.4 | async-start | bytes 4423680 | tf_op jit(solution)/shard_map/all_gather | solution.py:491
  11.9 213.1 %all-gather.8.cloned.1.call-start = ((), (), s32[]{:S(2)}) async-start(), calls=%async_computation.3 | async-start | bytes 12165120 | tf_op jit(solution)/shard_map/all_gather | solution.py:474
  12.8 298.1 %all-gather.12.cloned.1.call-start = ((), (), s32[]{:S(2)}) async-start(), calls=%async_computation.5 | async-start | bytes 10340352 | tf_op jit(solution)/shard_map/all_gather | solution.py:474
  13.4 383.4 %all-gather.14.cloned.1.call-start = ((), (), s32[]{:S(2)}) async-start(), calls=%async_computation.6 | async-start | bytes 10340352 | tf_op jit(solution)/shard_map/all_gather | solution.py:474
  14.0 619.9 %reduce-scatter.6.cloned.1.call-start = ((), (), s32[]{:S(2)}) async-start(), calls=%async_computation.9 | async-start | bytes 1769472 | tf_op jit(solution)/shard_map/reduce_scatter | solution.py:528
  17.1 105.9 %collective-permute-start = (bf16[512,1152]{1,0:T(8,128)(2,1)}, bf16[512,1152]{1,0:T(8,128)(2,1)}, u32[]{:S(2)}, u32[]{:S(2)}) collective-permute-start(bf16[512,1152]{1,0:T(8,128)(2,1)} %get-tuple-element.50), channel_id=1, source_target_pairs={{0,1},{1,0},{2,3},{3,2},{4,5},{5,4},{6,7},{7,6},{8,9},{9,8},{10,11... | collective-permute-start | bytes 3538952 | tf_op jit(solution)/shard_map/ppermute | solution.py:452
  21.6 5.1 copy-start.18
  21.6 5.1 copy-start.19
  21.6 5.1 copy-start.20
  21.6 5.2 copy-start.21
  21.6 5.2 copy-start.22
  21.7 5.2 copy-start.23
  21.7 5.2 copy-start.24
  21.7 88.2 %copy-start.27 = (u32[32]{0:T(128)S(1)}, u32[32]{0:T(128)}, u32[]{:S(2)}) copy-start(u32[32]{0:T(128)} %constant.148) | copy-start | bytes 388
  21.7 89.4 %copy-start.16 = (bf16[2152]{0:T(1024)(128)(2,1)S(1)}, bf16[2152]{0:T(1024)(128)(2,1)}, u32[]{:S(2)}) copy-start(bf16[2152]{0:T(1024)(128)(2,1)} %param.39) | copy-start | bytes 12916
  23.3 101.2 %collective-permute-start.1 = (bf16[512,1152]{1,0:T(8,128)(2,1)}, bf16[512,1152]{1,0:T(8,128)(2,1)}, u32[]{:S(2)}, u32[]{:S(2)}) collective-permute-start(bf16[512,1152]{1,0:T(8,128)(2,1)} %get-tuple-element.48), channel_id=1, source_target_pairs={{0,1},{1,0},{2,3},{3,2},{4,5},{5,4},{6,7},{7,6},{8,9},{9,8},{10,11... | collective-permute-start | bytes 3538952 | tf_op jit(solution)/shard_map/ppermute | solution.py:452
  109.0 15.4 %copy-start.6 = (f32[1152,8]{0,1:T(8,128)}, f32[1152,8]{0,1:T(8,128)S(1)}, u32[]{:S(2)}) copy-start(f32[1152,8]{0,1:T(8,128)S(1)} %reshape.120) | copy-start | bytes 110596
  124.5 7.4 copy-start
  530.5 133.4 %reduce-scatter.4.cloned.1.call-start = ((), (), s32[]{:S(2)}) async-start(), calls=%async_computation.8 | async-start | bytes 2654208 | tf_op jit(solution)/shard_map/reduce_scatter | solution.py:528
  622.1 101.5 %reduce-scatter.8.cloned.1.call-start = ((), (), s32[]{:S(2)}) async-start(), calls=%async_computation.10 | async-start | bytes 3342336 | tf_op jit(solution)/shard_map/reduce_scatter | solution.py:528
  626.0 203.1 %all-reduce.8.cloned.1.call-start = ((), (), s32[]{:S(2)}) async-start(), calls=%async_computation.11 | async-start | bytes 5177344 | tf_op jit(solution)/shard_map/psum | solution.py:529
  630.0 99.3 %collective-permute-start.2 = (bf16[512,1152]{1,0:T(8,128)(2,1)S(1)}, bf16[512,1152]{1,0:T(8,128)(2,1)S(1)}, u32[]{:S(2)}, u32[]{:S(2)}) collective-permute-start(bf16[512,1152]{1,0:T(8,128)(2,1)S(1)} %get-tuple-element.46), channel_id=1, source_target_pairs={{1,0},{0,1},{3,2},{2,3},{5,4},{4,5},{7,6},{6,7},{9,8},{8,9},{11,10... | collective-permute-start | bytes 3538952 | tf_op jit(solution)/shard_map/ppermute | solution.py:452
  633.1 97.3 %collective-permute-start.3 = (bf16[512,1152]{1,0:T(8,128)(2,1)S(1)}, bf16[512,1152]{1,0:T(8,128)(2,1)}, u32[]{:S(2)}, u32[]{:S(2)}) collective-permute-start(bf16[512,1152]{1,0:T(8,128)(2,1)S(1)} %fusion), channel_id=1, source_target_pairs={{1,0},{0,1},{3,2},{2,3},{5,4},{4,5},{7,6},{6,7},{9,8},{8,9},{11,10... | collective-permute-start | bytes 3538952 | tf_op jit(solution)/shard_map/ppermute | solution.py:452
  (18 other events, 43.0 us)
Sparse Core Ops, SparseCore 0:
  10.1 61.2 all-gather.15
  73.0 54.7 all-gather.9
  131.2 93.7 all-gather.7
  227.7 83.2 all-gather.11
  313.6 83.0 all-gather.13
  530.7 20.2 reduce-scatter.5
  622.2 41.6 reduce-scatter.3
  666.7 56.8 reduce-scatter.7
  728.0 101.0 all-reduce.7
